TPU v7x, 256 devices: a whole 4x4x8 slice. The times are simulated.
256 devices in a mesh: leaf: 4 (over y), row: 8 (over x, core), col: 8 (over z).
Axes of the slice: x: 4, y: 4, z: 8, core: 2. Of those that a mesh axis runs over, the one named last changes fastest.
Arguments:
- child_source: float32 [4, 4096, 384], P('leaf', 'col'), may hold values from -6 to 6
- middle_source: float32 [4, 4096, 384], P('leaf', 'col'), may hold values from -6 to 6
- root_source: float32 [16384, 384], P(('leaf', 'col')), may hold values from -6 to 6
- child_inverse: float32 [4, 4096, 4096], P('leaf', 'row', 'col'), may hold values from -0.09375 to 0.09375
- child_update: float32 [4, 2048, 4096], P('leaf', 'col', 'row'), may hold values from -0.09375 to 0.09375
- middle_inverse: float32 [4, 8192, 4096], P('leaf', 'row', 'col'), may hold values from -0.0625 to 0.0625
- middle_update: float32 [4, 2048, 8192], P('leaf', 'col', 'row'), may hold values from -0.0625 to 0.0625
- root_inverse: float32 [16384, 16384], P('row', ('leaf', 'col')), may hold values from -0.046875 to 0.046875
- child_diagmask: int32 [4, 32, 32], P('leaf', 'row', 'col'), may hold values 0 or 1
- child_updmask: int32 [4, 16, 32], P('leaf', 'col', 'row'), may hold values 0 or 1
- middle_diagmask: int32 [4, 64, 32], P('leaf', 'row', 'col'), may hold values 0 or 1
- middle_updmask: int32 [4, 16, 64], P('leaf', 'col', 'row'), may hold values 0 or 1
- root_diagmask: int32 [128, 128], P('row', ('leaf', 'col')), may hold values 0 or 1
- child_rowmap: int32 [4, 2048], replicated, may hold values from 0 to 8191
- middle_rowmap: int32 [2, 4096], replicated, may hold values from 0 to 16383
Outputs:
- child_solution: float32 [4, 4096, 384], P('leaf', 'row', 'col')
- middle_solution: float32 [4, 8192, 192], P('leaf', 'row', 'col')
- root_solution: float32 [16384, 384], P('row', 'col')
All inputs are finite; a program needn't handle non-finite values. No bound on the sum of `child_diagmask` or of `child_updmask` or of `middle_diagmask` or of `middle_updmask` or of `root_diagmask` on one device may be relied on, other than what follows from the above.
Results may differ from a plain program's by a relative error of at most 0.0001.
Values sent between devices are 32-bit elements; how exact they have to be, the bound alone decides.
A program may use at most 128 MiB of HBM per device.

v0:
```python
import jax
import jax.numpy as jnp
from jax import lax
from jax.sharding import PartitionSpec as P

BLK = 128
P0 = 4096
P1 = 8192
P2 = 16384
NRHS = 384


def swapped(value, axis, apart):
    mask = 2**apart
    pairs = [(source, source ^ mask) for source in range(lax.axis_size(axis))]
    return lax.ppermute(value, axis, pairs)


def expand(blocks):
    return jnp.repeat(jnp.repeat(blocks, BLK, axis=0), BLK, axis=1)


def keep_lower(pattern, row_first, col_first):
    rows_count, cols_count = pattern.shape
    row_ids = row_first + jnp.arange(rows_count, dtype=jnp.int32)[:, None]
    col_ids = col_first + jnp.arange(cols_count, dtype=jnp.int32)[None, :]
    keep = (row_ids == col_ids) | (row_ids > col_ids) & (pattern == 1)
    return expand(keep.astype(jnp.float32))


def masked_product(panel, keep, vector):
    return jnp.dot(
        panel * keep, vector, precision=lax.Precision.HIGHEST, preferred_element_type=jnp.float32
    )


def add_rows(target, incoming, targets, first_row):
    count = target.shape[0]
    local_rows = targets - first_row
    local_rows = jnp.where((local_rows >= 0) & (local_rows < count), local_rows, count)
    return target.at[local_rows].add(incoming, mode="drop")


def local(
    child_source,
    middle_source,
    root_source,
    child_inverse,
    child_update,
    middle_inverse,
    middle_update,
    root_inverse,
    child_diagmask,
    child_updmask,
    middle_diagmask,
    middle_updmask,
    root_diagmask,
    child_rowmap,
    middle_rowmap,
):
    leaf_index = lax.axis_index("leaf")
    row_index = lax.axis_index("row")
    col_index = lax.axis_index("col")
    n_leaf = lax.axis_size("leaf")
    n_row = lax.axis_size("row")
    n_col = lax.axis_size("col")
    half = leaf_index % 2
    couple = leaf_index // 2
    keep_child = keep_lower(
        child_diagmask[0], row_index * (P0 // n_row // BLK), col_index * (P0 // n_col // BLK)
    )
    ukeep_child = expand(child_updmask[0].astype(jnp.float32))
    middle_first = half * (P1 // 2) + col_index * (P1 // 2 // n_col)
    keep_middle = keep_lower(
        middle_diagmask[0], row_index * (P1 // n_row // BLK), middle_first // BLK
    )
    ukeep_middle = expand(middle_updmask[0].astype(jnp.float32))
    root_count = P2 // (n_leaf * n_col)
    root_first = (leaf_index * n_col + col_index) * root_count
    keep_root = keep_lower(root_diagmask, row_index * (P2 // n_row // BLK), root_first // BLK)
    pair_targets = lax.dynamic_slice_in_dim(child_rowmap, 2 * couple, 2, 0).reshape(-1)
    root_targets = middle_rowmap.reshape(-1)
    source_now = child_source[0]
    child_value = lax.psum(masked_product(child_inverse[0], keep_child, source_now), "col")
    child_lift = lax.psum(masked_product(child_update[0], ukeep_child, child_value), "row")
    middle_own = middle_source[0]
    mine = lax.all_gather(child_lift, "col", axis=0, tiled=True)
    sibling = swapped(mine, "leaf", 0)
    ordered = jnp.where(
        half == 0, jnp.concatenate([mine, sibling], 0), jnp.concatenate([sibling, mine], 0)
    )
    middle_rhs = add_rows(middle_own, ordered, pair_targets, middle_first)
    summed = lax.psum(masked_product(middle_inverse[0], keep_middle, middle_rhs), "col")
    middle_value = summed + swapped(summed, "leaf", 0)
    middle_lift = lax.psum(masked_product(middle_update[0], ukeep_middle, middle_value), "row")
    everyone = lax.all_gather(middle_lift, ("leaf", "col"), axis=0, tiled=True)
    root_rhs = add_rows(root_source, everyone, root_targets, root_first)
    root_partial = masked_product(root_inverse, keep_root, root_rhs)
    child_value, middle_value, root_partial = (child_value, middle_value, root_partial)
    share_width = NRHS // n_col
    root_value = lax.psum(root_partial, ("leaf", "col"))
    root_out = lax.dynamic_slice_in_dim(root_value, col_index * share_width, share_width, 1)
    child_out = lax.dynamic_slice_in_dim(child_value, col_index * share_width, share_width, 1)
    middle_width = NRHS // 2 // n_col
    middle_out = lax.dynamic_slice_in_dim(
        middle_value, half * (NRHS // 2) + col_index * middle_width, middle_width, 1
    )
    return (child_out[None], middle_out[None], root_out)


def solution(mesh):
    placed = (
        P("leaf", "col", None),
        P("leaf", "col", None),
        P(("leaf", "col"), None),
        P("leaf", "row", "col"),
        P("leaf", "col", "row"),
        P("leaf", "row", "col"),
        P("leaf", "col", "row"),
        P("row", ("leaf", "col")),
        P("leaf", "row", "col"),
        P("leaf", "col", "row"),
        P("leaf", "row", "col"),
        P("leaf", "col", "row"),
        P("row", ("leaf", "col")),
        P(),
        P(),
    )
    return jax.shard_map(
        local,
        mesh=mesh,
        in_specs=placed,
        out_specs=(P("leaf", "row", "col"), P("leaf", "row", "col"), P("row", "col")),
        check_vma=False,
    )
```

profile of v0, /device:TPU:2, one launch (start us, length us, event | category | flops | bytes accessed | tf_op | source)
XLA Modules:
  0.0 835.5 jit_solution(5975123913899786149)
XLA Ops:
  9.1 4.0 fusion.15
  13.2 77.8 %all-reduce.6.cloned.1.call-done = f32[512,384]{1,0:T(8,128)} async-done(((f32[512,384]{1,0:T(8,128)}), f32[512,384]{1,0:T(8,128)}) %all-reduce.6.cloned.1.call-update) | async-done | bytes 786448 | tf_op jit(solution)/shard_map/psum | solution.py:84
  91.3 2.9 fusion.19
  94.3 61.8 %all-reduce.8.cloned.1.call-done = f32[256,384]{1,0:T(8,128)} async-done(((f32[256,384]{1,0:T(8,128)}), f32[256,384]{1,0:T(8,128)}) %all-reduce.8.cloned.1.call-update) | async-done | bytes 393232 | tf_op jit(solution)/shard_map/psum | solution.py:85
  156.2 48.1 %all-gather.3.cloned.1.call-done = f32[2048,384]{1,0:T(8,128)} async-done(((f32[256,384]{1,0:T(8,128)}), f32[2048,384]{1,0:T(8,128)}) %all-gather.3.cloned.1.call-update) | async-done | bytes 3145744 | tf_op jit(solution)/shard_map/all_gather | solution.py:87
  204.3 1.5 collective-permute-start
  206.1 68.1 %collective-permute-done = f32[2048,384]{1,0:T(8,128)} collective-permute-done((f32[2048,384]{1,0:T(8,128)}, f32[2048,384]{1,0:T(8,128)}, u32[]{:S(2)}, u32[]{:S(2)}) %collective-permute-start) | collective-permute-done | bytes 3145760 | tf_op jit(solution)/shard_map/ppermute | solution.py:16
  274.2 27.4 %scatter_custom_fusion = f32[512,384]{1,0:T(8,128)S(1)} fusion(f32[512,384]{1,0:T(8,128)S(1)} %bitcast.81, s32[4096]{0:T(1024)S(1)} %bitcast.92, f32[2048,384]{1,0:T(8,128)} %collective-permute-done, f32[]{:T(128)} %constant.91, f32[2048,384]{1,0:T(8,128)} %all-gather.3.cloned.1.call-done, pred[]{:T(512)S(6)} %eq.76), kind=kCustom, calls=%fused_computation.3 | custom fusion | flops 6291456 | bytes 7077893 | tf_op jit(solution)/shard_map/scatter-add | solution.py:41
  301.7 1.2 broadcast_in_dim.52
  303.3 4.6 fusion.9
  307.9 77.6 %all-reduce.10.cloned.1.call-done = f32[1024,384]{1,0:T(8,128)} async-done(((f32[1024,384]{1,0:T(8,128)}), f32[1024,384]{1,0:T(8,128)}) %all-reduce.10.cloned.1.call-update) | async-done | bytes 1572880 | tf_op jit(solution)/shard_map/psum | solution.py:93
  385.5 1.5 collective-permute-start.1
  387.0 31.2 %collective-permute-done.1 = f32[1024,384]{1,0:T(8,128)S(1)} collective-permute-done((f32[1024,384]{1,0:T(8,128)}, f32[1024,384]{1,0:T(8,128)S(1)}, u32[]{:S(2)}, u32[]{:S(2)}) %collective-permute-start.1) | collective-permute-done | bytes 1572896 | tf_op jit(solution)/shard_map/ppermute | solution.py:16
  418.2 1.6 add.142
  420.2 3.9 fusion.12
  424.2 61.9 %all-reduce.12.cloned.1.call-done = f32[256,384]{1,0:T(8,128)} async-done(((f32[256,384]{1,0:T(8,128)}), f32[256,384]{1,0:T(8,128)}) %all-reduce.12.cloned.1.call-update) | async-done | bytes 393232 | tf_op jit(solution)/shard_map/psum | solution.py:95
  486.6 123.4 %all-gather.5.cloned.1.call-done = f32[8192,384]{1,0:T(8,128)} async-done(((f32[256,384]{1,0:T(8,128)}), f32[8192,384]{1,0:T(8,128)}) %all-gather.5.cloned.1.call-update) | async-done | bytes 12582928 | tf_op jit(solution)/shard_map/all_gather | solution.py:96
  610.0 49.3 %scatter_fusion = f32[512,384]{1,0:T(8,128)S(1)} fusion(f32[512,384]{1,0:T(8,128)S(1)} %copy-done.1, s32[8192]{0:T(1024)S(1)} %bitcast.88, f32[8192,384]{1,0:T(8,128)} %all-gather.5.cloned.1.call-done), kind=kCustom, calls=%fused_computation.1 | custom fusion | flops 3145728 | bytes 37781504 | tf_op jit(solution)/shard_map/scatter-add | solution.py:41
  659.4 4.7 broadcast_in_dim.57
  664.1 7.2 fusion.6
  671.3 1.2 constant_dynamic-slice_fusion.2
  673.5 0.8 copy.22
  674.3 152.6 %all-reduce.14.cloned.1.call-done = f32[2048,384]{0,1:T(8,128)} async-done(((f32[2048,384]{0,1:T(8,128)}), f32[2048,384]{0,1:T(8,128)}) %all-reduce.14.cloned.1.call-update) | async-done | bytes 3145744 | tf_op jit(solution)/shard_map/psum | solution.py:101
  826.9 1.8 constant_dynamic-slice_fusion
  (69 shorter events, 4.8 us)
Async XLA Ops:
  7.2 1.9 copy-start
  7.2 0.8 copy-start.8
  7.2 83.8 %all-reduce.6.cloned.1.call-start = ((), (), s32[]{:S(2)}) async-start(), calls=%async_computation | async-start | bytes 1572864 | tf_op jit(solution)/shard_map/psum | solution.py:84
  8.6 4.6 copy-start.11
  9.1 82.2 %copy-start.5 = (f32[1,256,512]{2,1,0:T(8,128)S(1)}, f32[1,256,512]{2,1,0:T(8,128)}, u32[]{:S(2)}) copy-start(f32[1,256,512]{2,1,0:T(8,128)} %param.19) | copy-start | bytes 1572868
  13.1 192.7 %copy-start.7 = (s32[4,2048]{1,0:T(4,128)S(1)}, s32[4,2048]{1,0:T(4,128)}, u32[]{:S(2)}) copy-start(s32[4,2048]{1,0:T(4,128)} %param.28) | copy-start | bytes 98308
  13.1 192.8 %copy-start.9 = (s32[1,8,4]{1,2,0:T(4,128)S(1)}, s32[1,8,4]{1,2,0:T(4,128)}, u32[]{:S(2)}) copy-start(s32[1,8,4]{1,2,0:T(4,128)} %param.25) | copy-start | bytes 388
  13.1 261.1 %copy-start.3 = (f32[1,512,384]{2,1,0:T(8,128)S(1)}, f32[1,512,384]{2,1,0:T(8,128)}, u32[]{:S(2)}) copy-start(f32[1,512,384]{2,1,0:T(8,128)} %param.16) | copy-start | bytes 2359300
  13.1 143.0 %all-reduce.8.cloned.1.call-start = ((), (), s32[]{:S(2)}) async-start(), calls=%async_computation.1 | async-start | bytes 786432 | tf_op jit(solution)/shard_map/psum | solution.py:85
  94.3 110.0 %all-gather.3.cloned.1.call-start = ((), (), s32[]{:S(2)}) async-start(), calls=%async_computation.2 | async-start | bytes 3538944 | tf_op jit(solution)/shard_map/all_gather | solution.py:87
  156.1 229.4 %all-reduce.10.cloned.1.call-start = ((), (), s32[]{:S(2)}) async-start(), calls=%async_computation.3 | async-start | bytes 3145728 | tf_op jit(solution)/shard_map/psum | solution.py:93
  204.3 69.9 %collective-permute-start = (f32[2048,384]{1,0:T(8,128)}, f32[2048,384]{1,0:T(8,128)}, u32[]{:S(2)}, u32[]{:S(2)}) collective-permute-start(f32[2048,384]{1,0:T(8,128)} %all-gather.3.cloned.1.call-done), channel_id=1, source_target_pairs={{0,64},{64,0},{128,192},{192,128},{1,65},{65,1},{129,193},{193,129... | collective-permute-start | bytes 9437192 | tf_op jit(solution)/shard_map/ppermute | solution.py:16
  301.7 1.6 copy-start.4
  303.3 83.7 %copy-start.12 = (s32[1,2,8]{2,1,0:T(2,128)S(1)}, s32[1,2,8]{2,1,0:T(2,128)}, u32[]{:S(2)}) copy-start(s32[1,2,8]{2,1,0:T(2,128)} %param.26) | copy-start | bytes 196
  307.9 178.3 %all-reduce.12.cloned.1.call-start = ((), (), s32[]{:S(2)}) async-start(), calls=%async_computation.4 | async-start | bytes 786432 | tf_op jit(solution)/shard_map/psum | solution.py:95
  385.5 32.7 %collective-permute-start.1 = (f32[1024,384]{1,0:T(8,128)}, f32[1024,384]{1,0:T(8,128)S(1)}, u32[]{:S(2)}, u32[]{:S(2)}) collective-permute-start(f32[1024,384]{1,0:T(8,128)} %all-reduce.10.cloned.1.call-done), channel_id=1, source_target_pairs={{0,64},{64,0},{128,192},{192,128},{1,65},{65,1},{129,193},{193,129... | collective-permute-start | bytes 4718600 | tf_op jit(solution)/shard_map/ppermute | solution.py:16
  419.9 66.4 %copy-start.6 = (s32[2,4096]{1,0:T(2,128)S(1)}, s32[2,4096]{1,0:T(2,128)}, u32[]{:S(2)}) copy-start(s32[2,4096]{1,0:T(2,128)} %param.29) | copy-start | bytes 98308
  419.9 66.5 %copy-start.10 = (s32[16,4]{0,1:T(4,128)S(1)}, s32[16,4]{0,1:T(4,128)}, u32[]{:S(2)}) copy-start(s32[16,4]{0,1:T(4,128)} %param.27) | copy-start | bytes 772
  419.9 190.1 %copy-start.1 = (f32[512,384]{1,0:T(8,128)S(1)}, f32[512,384]{1,0:T(8,128)}, u32[]{:S(2)}) copy-start(f32[512,384]{1,0:T(8,128)} %param.17) | copy-start | bytes 2359300
  424.2 185.8 %all-gather.5.cloned.1.call-start = ((), (), s32[]{:S(2)}) async-start(), calls=%async_computation.5 | async-start | bytes 12976128 | tf_op jit(solution)/shard_map/all_gather | solution.py:96
  486.2 340.7 %all-reduce.14.cloned.1.call-start = ((), (), s32[]{:S(2)}) async-start(), calls=%async_computation.6 | async-start | bytes 6291456 | tf_op jit(solution)/shard_map/psum | solution.py:101
  659.3 4.8 copy-start.2
Sparse Core Ops, SparseCore 0:
  13.3 77.6 all-reduce.5
  94.4 61.6 all-reduce.7
  157.9 46.3 all-gather.2
  308.0 77.4 all-reduce.9
  424.3 61.7 all-reduce.11
  488.9 121.0 all-gather.4
  671.4 155.4 all-reduce.13
where the time goes:
time: 836 us; the launch traced here: 835 us
  waiting for transfers between devices  703 us (84%)
  other arithmetic  78.8 us (9%)
  matrix products  22.6 us (3%)
  between operations  14.5 us (2%)
  local copies, waits for them, and re-layouts  13.7 us (2%)
    psum x1, waiting for transfers between devices, local(): root_value = lax.psum(root_partial, ('leaf', 'col'))  153 us
    all_gather x1, waiting for transfers between devices, local(): everyone = lax.all_gather(middle_lift, ('leaf', 'col'), axis=0, tiled=True)  123 us
    ppermute x2, waiting for transfers between devices, swapped(): return lax.ppermute(value, axis, pairs)  99.4 us
    psum x1, waiting for transfers between devices, local(): lax.psum(masked_product(child_inverse[0], keep_child, source_now), 'col')  77.8 us
    psum x1, waiting for transfers between devices, local(): lax.psum(masked_product(middle_inverse[0], keep_middle, middle_rhs), 'col')  77.6 us
    scatter-add x2, other arithmetic, add_rows(): return target.at[local_rows].add(incoming, mode='drop')  76.8 us
    psum x1, waiting for transfers between devices, local(): lax.psum(masked_product(middle_update[0], ukeep_middle, middle_value), 'r...  61.9 us
    psum x1, waiting for transfers between devices, local(): lax.psum(masked_product(child_update[0], ukeep_child, child_value), 'row')  61.8 us
  transfers between devices with their start and end apart: 9, of which 9 were waited for; matrix products, arithmetic and copies ran while one was open for 0% of the time, Pallas kernels for 0%

commit v1 on v0

v1 whole, which is shorter than its diff:
```python
import functools
from types import SimpleNamespace

import jax
import jax.numpy as jnp
from jax import lax
from jax.experimental import pallas as pl
from jax.experimental.pallas import tpu as pltpu
from jax.sharding import PartitionSpec as P

BLK = 128
BATCHES = 3
COPIES = 256
TILE = 256
MESH = pl.DeviceIdType.MESH
F32 = jnp.float32
BF16 = jnp.bfloat16
NT = (((1,), (1,)), ((), ()))


def run(streams, filler=None):
    live = list(streams)
    while live:
        for stream in list(live):
            if next(stream, StopIteration) is StopIteration:
                live.remove(stream)
        if filler is not None:
            filler.step()


class Filler:
    def __init__(self):
        self.tasks = []

    def add(self, name, pieces):
        self.tasks.append((name, pieces))

    def step(self):
        while self.tasks:
            name, pieces = self.tasks[0]
            if next(pieces, StopIteration) is StopIteration:
                self.tasks.pop(0)
            else:
                return

    def need(self, name):
        while any(task[0] is name for task in self.tasks):
            self.step()


class Links:
    def __init__(self, send_sems, recv_sems):
        self.send_sems = send_sems
        self.recv_sems = recv_sems
        self.count = 0
        self.sent = []

    def send(self, source, landing, target):
        index = self.count
        self.count += 1
        copy = pltpu.make_async_remote_copy(
            src_ref=source,
            dst_ref=landing,
            send_sem=self.send_sems.at[index],
            recv_sem=self.recv_sems.at[index],
            device_id=target,
            device_id_type=MESH,
        )
        copy.start()
        self.sent.append(copy)
        return copy

    def close(self):
        for copy in self.sent:
            copy.wait_send()


class Ring:
    def __init__(self, index, length, device):
        self.index = index
        self.length = length
        self.device = device

    def at(self, offset):
        return lax.rem(self.index + offset + 2 * self.length, self.length)


def ring_reduce_scatter(links, ring, longer, part, landing):
    far = ring.length // 2
    reach = {longer: far, -longer: far - 1}
    before = {}
    for step in range(far + 1):
        if step > 0:
            yield
        for way in (longer, -longer):
            hops = reach[way] - step
            if hops < 0:
                continue
            term = part(ring.at(way * hops))
            if step > 0:
                before[way].wait_recv()
                term[...] = term[...] + landing(way, step - 1)[...]
            if hops > 0:
                before[way] = links.send(term, landing(way, step), ring.device(ring.at(way)))


def ring_all_gather(links, ring, longer, part, arrived=None):
    far = ring.length // 2
    reach = {longer: far, -longer: far - 1}
    before = {}
    for step in range(far + 1):
        if step > 0:
            yield
        new = [ring.index] if step == 0 else []
        for way in (longer, -longer):
            if step > reach[way]:
                continue
            chunk = ring.at(-way * step)
            if step > 0:
                before[way].wait_recv()
                new.append(chunk)
            if step < reach[way]:
                before[way] = links.send(part(chunk), part(chunk), ring.device(ring.at(way)))
        if arrived is not None:
            for chunk in new:
                arrived(chunk)


def split(value):
    high = value.astype(BF16)
    return high, (value - high.astype(F32)).astype(BF16)


def product(left, panel_high, panel_low, out, depth, shape):
    count = left.shape[0] // 2

    def tile(j, carry):
        rows = pl.ds(pl.multiple_of(j * TILE, TILE), TILE)
        both = lax.dot_general(left[:, :depth], panel_high[rows, :], NT, preferred_element_type=F32)
        last = lax.dot_general(
            left[:count, :depth], panel_low[rows, :], NT, preferred_element_type=F32
        )
        out(j)[...] = (both[:count] + both[count:] + last).reshape(shape)
        return carry

    lax.fori_loop(0, panel_high.shape[0] // TILE, tile, 0)


def kernel(sizes, names, *refs):
    ref = SimpleNamespace(**dict(zip(names, refs)))
    n_leaf, n_row, n_col, p0, p1, p2, nrhs = sizes
    n_x = n_row // 2
    leaf, row, col = lax.axis_index("leaf"), lax.axis_index("row"), lax.axis_index("col")
    half, couple = lax.rem(leaf, 2), lax.div(leaf, 2)
    x, core = lax.div(row, 2), lax.rem(row, 2)
    ring_y = Ring(leaf, n_leaf, lambda i: {"leaf": i})
    ring_z = Ring(col, n_col, lambda i: {"col": i})
    ring_x = Ring(x, n_x, lambda i: {"row": i * 2 + core})
    pair = {"leaf": couple * 2 + 1 - half}
    twin = {"row": x * 2 + 1 - core}
    links = Links(ref.send_sems, ref.recv_sems)
    width = nrhs // BATCHES
    share, cshare, mshare = width // n_row, width // n_col, width // 2 // n_col
    groups = width // mshare

    loads = {}
    for index, (source, landing) in enumerate(
        (
            (ref.child_source.at[0], ref.v_child_source),
            (ref.child_inverse.at[0], ref.v_child_inverse),
            (ref.child_update.at[0], ref.v_child_update),
            (ref.middle_source.at[0], ref.v_middle_source),
            (ref.middle_inverse.at[0], ref.v_middle_inverse),
            (ref.middle_update.at[0], ref.v_middle_update),
            (ref.root_source, ref.v_root_source),
            (ref.root_inverse, ref.v_root_inverse),
        )
    ):
        loads[id(landing)] = pltpu.make_async_copy(source, landing, ref.load_sems.at[index])
        loads[id(landing)].start()

    barrier = pltpu.get_barrier_semaphore()
    friends = [twin]
    for ring in (ring_x, ring_y, ring_z):
        friends += [ring.device(ring.at(1)), ring.device(ring.at(-1))]
    for friend in friends:
        pl.semaphore_signal(barrier, inc=1, device_id=friend, device_id_type=MESH)

    def prepare(panel, high, low, mask, first_row, first_col, pieces):
        blocks, across = panel.shape[0] // BLK, panel.shape[1] // BLK
        loads[id(panel)].wait()

        def body(i, carry):
            rows = pl.ds(pl.multiple_of(i * BLK, BLK), BLK)
            for j in range(across):
                kept = mask(i, j) == 1
                if first_row is not None:
                    down, right = first_row + i, first_col + j
                    kept = (down == right) | ((down > right) & kept)
                columns = slice(j * BLK, (j + 1) * BLK)
                block = panel[rows, columns] * kept.astype(F32)
                top, rest = split(block)
                high[rows, columns] = top
                low[rows, columns] = rest
            return carry

        for piece in range(pieces):
            lax.fori_loop(blocks * piece // pieces, blocks * (piece + 1) // pieces, body, 0)
            yield

    def flip(source, flipped):
        loads[id(source)].wait()
        for part in range(source.shape[0] // 256):
            rows = slice(part * 256, (part + 1) * 256)
            flipped[:, :, :, rows] = source[rows, :].T.reshape(groups, BATCHES, mshare, 256)
            yield

    def one_hot(out, rowmap, first, pieces):
        count = out.shape[0]
        place = lax.broadcasted_iota(jnp.int32, out.shape[1:], 0) + first

        def body(k, carry):
            out[k] = (rowmap(k) == place).astype(F32).astype(BF16)
            return carry

        for piece in range(pieces):
            lax.fori_loop(count * piece // pieces, count * (piece + 1) // pieces, body, 0)
            yield

    def child_map(k):
        columns = pl.ds(pl.multiple_of(lax.rem(k, n_col) * TILE, TILE), TILE)
        return ref.child_rowmap[pl.ds(2 * couple + lax.div(k, n_col), 1), columns]

    def middle_map(k):
        owner = lax.div(k, n_col)
        start = (lax.rem(owner, 2) * n_col + lax.rem(k, n_col)) * TILE
        columns = pl.ds(pl.multiple_of(start, TILE), TILE)
        return ref.middle_rowmap[pl.ds(lax.div(owner, 2), 1), columns]

    middle_first = (half * n_col + col) * (p1 // 2 // n_col)
    root_first = (leaf * n_col + col) * (p2 // n_leaf // n_col)
    filler = Filler()
    filler.add(ref.child_update,
        prepare(ref.v_child_update, ref.h_child_update, ref.l_child_update, lambda i, j: ref.child_updmask[0, i, j], None, None, 1),
    )
    filler.add(ref.hot_middle, one_hot(ref.hot_middle, child_map, middle_first, 4))
    filler.add(ref.middle_source, flip(ref.v_middle_source, ref.t_middle_source))
    filler.add(ref.middle_inverse,
        prepare(ref.v_middle_inverse, ref.h_middle_inverse, ref.l_middle_inverse,
            lambda i, j: ref.middle_diagmask[0, i, j],
            row * (p1 // n_row // BLK),
            lax.div(middle_first, BLK),
            4,
        ),
    )
    filler.add(ref.middle_update,
        prepare(ref.v_middle_update, ref.h_middle_update, ref.l_middle_update, lambda i, j: ref.middle_updmask[0, i, j], None, None, 2),
    )
    filler.add(ref.root_source, flip(ref.v_root_source, ref.t_root_source))
    filler.add(ref.hot_root, one_hot(ref.hot_root, middle_map, root_first, 8))
    filler.add(ref.root_inverse,
        prepare(ref.v_root_inverse, ref.h_root_inverse, ref.l_root_inverse,
            lambda i, j: ref.root_diagmask[i, j],
            row * (p2 // n_row // BLK),
            lax.div(root_first, BLK),
            8,
        ),
    )

    for _ in prepare(ref.v_child_inverse, ref.h_child_inverse, ref.l_child_inverse,
        lambda i, j: ref.child_diagmask[0, i, j],
        row * (p0 // n_row // BLK),
        col * (p0 // n_col // BLK),
        1,
    ):
        pass
    for _ in flip(ref.v_child_source, ref.t_child_source):
        pass

    def chain(b):
        longer = 1 if b == 1 else -1
        left = ref.left.at[b]

        def fill_left(value, columns):
            high, low = split(value)
            left[:width, columns] = high
            left[width:, columns] = low

        def lift_reduce(lift, twin_land, land):
            copy = links.send(lift.at[:, 1 - core], twin_land, twin)
            yield
            copy.wait_recv()
            lift[:, core] = lift[:, core] + twin_land[...]
            yield from ring_reduce_scatter(
                links,
                ring_x,
                longer,
                lambda d: lift.at[d, core],
                lambda way, step: land.at[(way + 1) // 2, step],
            )

        def row_gather(buffer):
            copies = []

            def arrived(d):
                copies.append(links.send(buffer.at[d, core], buffer.at[d, core], twin))

            yield from ring_all_gather(
                links, ring_x, longer, lambda d: buffer.at[d, core], arrived
            )
            yield
            for copy in copies:
                copy.wait_recv()

        def add_block(total, block, hot):
            high = block.astype(BF16).astype(F32)
            both = jnp.concatenate([high, block - high], axis=0).astype(BF16)
            total[...] += lax.dot_general(both, hot, NT, preferred_element_type=F32)

        depth = p0 // n_col
        fill_left(ref.t_child_source[:, b].reshape(width, depth), slice(0, depth))
        terms = ref.child_terms.at[b]
        product(
            left,
            ref.h_child_inverse,
            ref.l_child_inverse,
            lambda j: terms.at[j],
            depth,
            (n_col, cshare, TILE),
        )
        if b == 0:
            pl.semaphore_wait(barrier, len(friends))
        yield from ring_reduce_scatter(
            links,
            ring_z,
            longer,
            lambda d: terms.at[:, d],
            lambda way, step: ref.child_land.at[b, (way + 1) // 2, step],
        )
        value = ref.child_value.at[b]
        value[:, col] = terms[:, col]
        ref.child_out[:, :, b] = terms[:, col].reshape(p0 // n_row // TILE, 2, mshare, TILE)
        yield from ring_all_gather(links, ring_z, longer, lambda d: value.at[:, d])

        filler.need(ref.child_update)
        for j in range(p0 // n_row // TILE):
            fill_left(value[j].reshape(width, TILE), slice(j * TILE, (j + 1) * TILE))
        lift = ref.child_lift.at[b]
        product(
            left,
            ref.h_child_update,
            ref.l_child_update,
            lambda j: lift,
            p0 // n_row,
            (n_x, 2, share, TILE),
        )
        yield from lift_reduce(lift, ref.child_twin.at[b], ref.child_lift_land.at[b])

        got = ref.child_lifts.at[b]
        got[half, col] = lift[x, core]
        copy = links.send(got.at[half, col], got.at[half, col], pair)
        filler.need(ref.hot_middle)
        total = ref.middle_total.at[b]
        total[...] = jnp.zeros_like(total)
        yield
        copy.wait_recv()

        def child_arrived(d):
            for which in range(2):
                add_block(total, got[which, d], ref.hot_middle[which * n_col + d])

        yield from ring_all_gather(links, ring_z, longer, lambda d: got.at[:, d], child_arrived)
        filler.need(ref.middle_source)
        rhs = ref.middle_rhs.at[b]
        source = ref.t_middle_source[pl.ds(2 * row, 2), b].reshape(share, -1)
        rhs[x, core] = source + total[:share] + total[share:]
        yield from row_gather(rhs)

        filler.need(ref.middle_inverse)
        depth = p1 // 2 // n_col
        fill_left(rhs[...].reshape(width, depth), slice(0, depth))
        mid = ref.middle_terms.at[b]
        tiles = p1 // n_row // TILE
        product(
            left,
            ref.h_middle_inverse,
            ref.l_middle_inverse,
            lambda j: mid.at[j],
            depth,
            (2, n_col, mshare, TILE),
        )
        yield from ring_reduce_scatter(
            links,
            ring_z,
            longer,
            lambda d: mid.at[:, :, d],
            lambda way, step: ref.middle_land.at[b, (way + 1) // 2, step],
        )
        copy = links.send(mid.at[:, 1 - half, col], ref.middle_pair.at[b], pair)
        yield
        copy.wait_recv()
        solved = ref.middle_value.at[b]
        summed = mid[:, half, col] + ref.middle_pair[b]
        solved[:, half, col] = summed
        ref.middle_out[:, b] = summed
        copy = links.send(solved.at[:, half, col], solved.at[:, half, col], pair)
        yield
        copy.wait_recv()
        yield from ring_all_gather(links, ring_z, longer, lambda d: solved.at[:, :, d])

        filler.need(ref.middle_update)
        for j in range(tiles):
            fill_left(solved[j].reshape(width, TILE), slice(j * TILE, (j + 1) * TILE))
        lift2 = ref.middle_lift.at[b]
        product(
            left,
            ref.h_middle_update,
            ref.l_middle_update,
            lambda j: lift2,
            p1 // n_row,
            (n_x, 2, share, TILE),
        )
        yield from lift_reduce(lift2, ref.middle_twin.at[b], ref.middle_lift_land.at[b])

        every = ref.middle_lifts.at[b]
        every[leaf, col] = lift2[x, core]
        yield from ring_all_gather(links, ring_y, longer, lambda d: every.at[d, col])
        filler.need(ref.hot_root)
        total2 = ref.root_total.at[b]
        total2[...] = jnp.zeros_like(total2)

        def middle_arrived(d):
            for which in range(n_leaf):
                add_block(total2, every[which, d], ref.hot_root[which * n_col + d])

        yield from ring_all_gather(links, ring_z, longer, lambda d: every.at[:, d], middle_arrived)
        filler.need(ref.root_source)
        rhs2 = ref.root_rhs.at[b]
        source2 = ref.t_root_source[pl.ds(2 * row, 2), b].reshape(share, -1)
        rhs2[x, core] = source2 + total2[:share] + total2[share:]
        yield from row_gather(rhs2)

        filler.need(ref.root_inverse)
        depth = p2 // n_leaf // n_col
        fill_left(rhs2[...].reshape(width, depth), slice(0, depth))
        root = ref.root_terms.at[b]
        each = p2 // n_row // TILE // n_leaf
        product(
            left,
            ref.h_root_inverse,
            ref.l_root_inverse,
            lambda j: root.at[j],
            depth,
            (n_col, cshare, TILE),
        )
        if b == 0:
            yield from ring_reduce_scatter(
                links,
                ring_z,
                longer,
                lambda d: root.at[:, d],
                lambda way, step: ref.root_land_az.at[(way + 1) // 2, step],
            )
            yield from ring_reduce_scatter(
                links,
                ring_y,
                longer,
                lambda d: root.at[pl.ds(d * each, each), col],
                lambda way, step: ref.root_land_ay.at[(way + 1) // 2, step],
            )
        else:
            yield from ring_reduce_scatter(
                links,
                ring_y,
                longer,
                lambda d: root.at[pl.ds(d * each, each)],
                lambda way, step: ref.root_land_by.at[b - 1, (way + 1) // 2, step],
            )
            yield from ring_reduce_scatter(
                links,
                ring_z,
                longer,
                lambda d: root.at[pl.ds(leaf * each, each), d],
                lambda way, step: ref.root_land_bz.at[b - 1, (way + 1) // 2, step],
            )
        final = ref.root_out
        mine = root[pl.ds(leaf * each, each), col]
        final[pl.ds(leaf * each, each), :, b] = mine.reshape(each, 2, mshare, TILE)
        yield from ring_all_gather(
            links, ring_y, longer, lambda d: final.at[pl.ds(d * each, each), :, b]
        )

    run([chain(b) for b in range(BATCHES)], filler)
    assert links.count <= COPIES
    links.close()


def local(
    n_leaf,
    n_row,
    n_col,
    child_source,
    middle_source,
    root_source,
    child_inverse,
    child_update,
    middle_inverse,
    middle_update,
    root_inverse,
    child_diagmask,
    child_updmask,
    middle_diagmask,
    middle_updmask,
    root_diagmask,
    child_rowmap,
    middle_rowmap,
):
    given = dict(
        child_source=child_source,
        middle_source=middle_source,
        root_source=root_source,
        child_inverse=child_inverse,
        child_update=child_update,
        middle_inverse=middle_inverse,
        middle_update=middle_update,
        root_inverse=root_inverse,
        child_diagmask=child_diagmask,
        child_updmask=child_updmask,
        middle_diagmask=middle_diagmask,
        middle_updmask=middle_updmask,
        root_diagmask=root_diagmask,
        child_rowmap=child_rowmap,
        middle_rowmap=middle_rowmap,
    )
    nrhs = child_source.shape[2]
    p0 = child_inverse.shape[2] * n_col
    p1 = middle_inverse.shape[1] * n_row
    p2 = root_inverse.shape[0] * n_row
    sizes = (n_leaf, n_row, n_col, p0, p1, p2, nrhs)
    n_x = n_row // 2
    width = nrhs // BATCHES
    share, cshare, mshare = width // n_row, width // n_col, width // 2 // n_col
    groups = width // mshare
    reach_z, reach_y, reach_x = n_col // 2, n_leaf // 2, n_x // 2
    t0, t1, t2 = (p // n_row // TILE for p in (p0, p1, p2))
    scratch = dict(
        v_child_inverse=pltpu.VMEM(child_inverse.shape[-2:], F32),
        h_child_inverse=pltpu.VMEM(child_inverse.shape[-2:], BF16),
        l_child_inverse=pltpu.VMEM(child_inverse.shape[-2:], BF16),
        v_child_update=pltpu.VMEM(child_update.shape[-2:], F32),
        h_child_update=pltpu.VMEM(child_update.shape[-2:], BF16),
        l_child_update=pltpu.VMEM(child_update.shape[-2:], BF16),
        v_middle_inverse=pltpu.VMEM(middle_inverse.shape[-2:], F32),
        h_middle_inverse=pltpu.VMEM(middle_inverse.shape[-2:], BF16),
        l_middle_inverse=pltpu.VMEM(middle_inverse.shape[-2:], BF16),
        v_middle_update=pltpu.VMEM(middle_update.shape[-2:], F32),
        h_middle_update=pltpu.VMEM(middle_update.shape[-2:], BF16),
        l_middle_update=pltpu.VMEM(middle_update.shape[-2:], BF16),
        v_root_inverse=pltpu.VMEM(root_inverse.shape[-2:], F32),
        h_root_inverse=pltpu.VMEM(root_inverse.shape[-2:], BF16),
        l_root_inverse=pltpu.VMEM(root_inverse.shape[-2:], BF16),
        v_child_source=pltpu.VMEM(child_source.shape[-2:], F32),
        t_child_source=pltpu.VMEM((groups, BATCHES, mshare, child_source.shape[-2]), F32),
        v_middle_source=pltpu.VMEM(middle_source.shape[-2:], F32),
        t_middle_source=pltpu.VMEM((groups, BATCHES, mshare, middle_source.shape[-2]), F32),
        v_root_source=pltpu.VMEM(root_source.shape[-2:], F32),
        t_root_source=pltpu.VMEM((groups, BATCHES, mshare, root_source.shape[-2]), F32),
    )
    d1, d2 = p1 // 2 // n_col, p2 // n_leaf // n_col
    depth = max(p0 // n_col, p0 // n_row, d1, p1 // n_row, d2)
    scratch.update(left=pltpu.VMEM((BATCHES, 2 * width, depth), BF16))
    scratch.update(hot_middle=pltpu.VMEM((2 * n_col, d1, TILE), BF16))
    scratch.update(hot_root=pltpu.VMEM((n_leaf * n_col, d2, TILE), BF16))
    shapes = dict(
        child_terms=(BATCHES, t0, n_col, cshare, TILE),
        child_land=(BATCHES, 2, reach_z, t0, cshare, TILE),
        child_value=(BATCHES, t0, n_col, cshare, TILE),
        child_lift=(BATCHES, n_x, 2, share, TILE),
        child_twin=(BATCHES, n_x, share, TILE),
        child_lift_land=(BATCHES, 2, reach_x, share, TILE),
        child_lifts=(BATCHES, 2, n_col, share, TILE),
        middle_total=(BATCHES, 2 * share, d1),
        middle_rhs=(BATCHES, n_x, 2, share, d1),
        middle_terms=(BATCHES, t1, 2, n_col, mshare, TILE),
        middle_land=(BATCHES, 2, reach_z, t1, 2, mshare, TILE),
        middle_pair=(BATCHES, t1, mshare, TILE),
        middle_value=(BATCHES, t1, 2, n_col, mshare, TILE),
        middle_lift=(BATCHES, n_x, 2, share, TILE),
        middle_twin=(BATCHES, n_x, share, TILE),
        middle_lift_land=(BATCHES, 2, reach_x, share, TILE),
        middle_lifts=(BATCHES, n_leaf, n_col, share, TILE),
        root_total=(BATCHES, 2 * share, d2),
        root_rhs=(BATCHES, n_x, 2, share, d2),
        root_terms=(BATCHES, t2, n_col, cshare, TILE),
        root_land_az=(2, reach_z, t2, cshare, TILE),
        root_land_ay=(2, reach_y, t2 // n_leaf, cshare, TILE),
        root_land_by=(BATCHES - 1, 2, reach_y, t2 // n_leaf, n_col, cshare, TILE),
        root_land_bz=(BATCHES - 1, 2, reach_z, t2 // n_leaf, cshare, TILE),
    )
    for name, shape in shapes.items():
        scratch[name] = pltpu.VMEM(shape, F32)
    scratch.update(send_sems=pltpu.SemaphoreType.DMA((COPIES,)))
    scratch.update(recv_sems=pltpu.SemaphoreType.DMA((COPIES,)))
    scratch.update(load_sems=pltpu.SemaphoreType.DMA((8,)))
    outs = dict(
        child_out=(t0, 2, BATCHES, mshare, TILE),
        middle_out=(t1, BATCHES, mshare, TILE),
        root_out=(t2, 2, BATCHES, mshare, TILE),
    )
    vmem = pl.BlockSpec(memory_space=pltpu.VMEM)
    smem = pl.BlockSpec(memory_space=pltpu.SMEM)
    whole = pl.BlockSpec(memory_space=pl.ANY)
    child, middle, root = pl.pallas_call(
        functools.partial(kernel, sizes, tuple(given) + tuple(outs) + tuple(scratch)),
        out_shape=[jax.ShapeDtypeStruct(shape, F32) for shape in outs.values()],
        in_specs=[whole] * 8 + [smem] * 5 + [vmem] * 2,
        out_specs=[vmem] * 3,
        scratch_shapes=list(scratch.values()),
        compiler_params=pltpu.CompilerParams(
            collective_id=0, has_side_effects=True, vmem_limit_bytes=60 * 2**20
        ),
    )(*given.values())
    return tuple(
        blocks.reshape(*lead, blocks.shape[0], -1, TILE)
        .swapaxes(-1, -2)
        .reshape(*lead, blocks.shape[0] * TILE, -1)
        for blocks, lead in ((child, (1,)), (middle, (1,)), (root, ()))
    )


def solution(mesh):
    placed = (
        P("leaf", "col", None),
        P("leaf", "col", None),
        P(("leaf", "col"), None),
        P("leaf", "row", "col"),
        P("leaf", "col", "row"),
        P("leaf", "row", "col"),
        P("leaf", "col", "row"),
        P("row", ("leaf", "col")),
        P("leaf", "row", "col"),
        P("leaf", "col", "row"),
        P("leaf", "row", "col"),
        P("leaf", "col", "row"),
        P("row", ("leaf", "col")),
        P(),
        P(),
    )
    counts = (mesh.shape["leaf"], mesh.shape["row"], mesh.shape["col"])
    return jax.shard_map(
        functools.partial(local, *counts),
        mesh=mesh,
        in_specs=placed,
        out_specs=(P("leaf", "row", "col"), P("leaf", "row", "col"), P("row", "col")),
        check_vma=False,
    )
```

time: 836 us -> 204 us (0.24)
  waiting for transfers between devices: 703 us -> 0 us
  Pallas kernels: 0 us -> 195 us
  other arithmetic: 78.8 us -> 0 us
  matrix products: 22.6 us -> 0 us
  between operations: 14.5 us -> 0.64 us
    psum x5 -> x0, waiting for transfers between devices: 432 us -> none  [the longest x1 153 us: local(): root_value = lax.psum(root_partial, ('leaf', 'col'))]
    pallas_call x0 -> x1, Pallas kernels: none -> 195 us  [local(): pl.pallas_call(functools.partial(kernel, sizes, tuple(given) + tuple(outs...]
    all_gather x2 -> x0, waiting for transfers between devices: 172 us -> none  [the longest x1 123 us: local(): everyone = lax.all_gather(middle_lift, ('leaf', 'col'), axis=0, tiled=True)]
    ppermute x2 -> x0, waiting for transfers between devices: 99.4 us -> none  [swapped(): return lax.ppermute(value, axis, pairs)]
    scatter-add x2 -> x0, other arithmetic: 76.8 us -> none  [add_rows(): return target.at[local_rows].add(incoming, mode='drop')]
    dot_general x5 -> x0, matrix products: 22.6 us -> none  [masked_product(): jnp.dot(panel * keep, vector, precision=lax.Precision.HIGHEST, preferred_...]
  transfers between devices with their start and end apart: 9 -> 0, of which waited for: 9 -> 0; matrix products, arithmetic and copies ran while one was open for 0% -> 0% of each run, Pallas kernels for 0% -> 0%
where the time goes in v1:
time: 204 us
  Pallas kernels  195 us (96%)
  local copies, waits for them, and re-layouts  7.56 us (4%)
    pallas_call x1, Pallas kernels, local(): pl.pallas_call(functools.partial(kernel, sizes, tuple(given) + tuple(outs...  195 us
    reshape x3, local copies, waits for them, and re-layouts, local(): blocks.reshape(*lead, blocks.shape[0], -1, TILE).swapaxes(-1, -2)  4.85 us

profile of v1, /device:TPU:2, one launch (start us, length us, event | category | flops | bytes accessed | tf_op | source)
XLA Modules:
  0.0 203.5 jit_solution(13512000008314944335)
XLA Ops:
  0.6 1.3 copy.18.refs_10_
  2.0 1.4 copy.19.refs_12_
  3.3 195.3 %shard_map.166 = (f32[2,2,3,8,256]{4,3,2,1,0:T(8,128)}, f32[4,3,8,256]{3,2,1,0:T(8,128)}, f32[8,2,3,8,256]{4,3,2,1,0:T(8,128)}) custom-call(f32[1,512,384]{2,1,0:T(8,128)} %refs_0_.1, f32[1,512,384]{2,1,0:T(8,128)} %refs_1_.1, f32[512,384]{1,0:T(8,128)} %refs_2_.1, f32[1,512,512]{2,1,0:T(8,128)} %refs_3_.1, f32[1,256,512]{2,1,0:T(8,128)} %refs_4_.1, ...), custom_call_target="tpu_custom_call" | custom-call | tf_op jit(solution)/shard_map/pallas_call | solution.py:613
  198.7 1.5 copy.23
  200.2 1.5 copy.24
  201.8 1.8 copy.25

commit v2 on v1

--- a/solution.py
+++ b/solution.py
@@ -104,26 +104,77 @@
                 before[way] = links.send(term, landing(way, step), ring.device(ring.at(way)))
 
 
-def ring_all_gather(links, ring, longer, part, arrived=None):
-    far = ring.length // 2
-    reach = {longer: far, -longer: far - 1}
+def fold_reduce_scatter(links, ring, longer, part, landing):
     before = {}
-    for step in range(far + 1):
+    for step in range(4):
+        if step > 0:
+            yield
+        for way in (longer, -longer):
+            term = part(ring.at(way * (3 - step)))
+            if step > 0:
+                before[way].wait_recv()
+                term[...] = term[...] + landing((way + 1) // 2 * 3 + step - 1)[...]
+            if step == 1 and way == longer:
+                opposite.wait_recv()
+                term[...] = term[...] + landing(6)[...]
+            if step < 3:
+                before[way] = links.send(
+                    term, landing((way + 1) // 2 * 3 + step), ring.device(ring.at(way))
+                )
+        if step == 0:
+            opposite = links.send(
+                part(ring.at(4)), landing(6), ring.device(ring.at(2 * longer))
+            )
+
+
+def fold_all_gather(links, ring, longer, part, arrived=None):
+    before = {}
+    for step in range(4):
         if step > 0:
             yield
         new = [ring.index] if step == 0 else []
         for way in (longer, -longer):
-            if step > reach[way]:
-                continue
             chunk = ring.at(-way * step)
             if step > 0:
                 before[way].wait_recv()
                 new.append(chunk)
-            if step < reach[way]:
+            if step < 3:
                 before[way] = links.send(part(chunk), part(chunk), ring.device(ring.at(way)))
+        if step == 2:
+            chunk = ring.at(-longer * 2)
+            opposite = links.send(part(chunk), part(chunk), ring.device(ring.at(2 * longer)))
         if arrived is not None:
             for chunk in new:
                 arrived(chunk)
+    opposite.wait_recv()
+    if arrived is not None:
+        arrived(ring.at(4))
+
+
+def direct_reduce_scatter(links, ring, part, landing):
+    copies = []
+    for slot, offset in enumerate((2, 1, -1)):
+        target = ring.at(offset)
+        copies.append(links.send(part(target), landing(slot), ring.device(target)))
+    yield
+    term = part(ring.index)
+    for slot in (1, 2, 0):
+        copies[slot].wait_recv()
+        term[...] = term[...] + landing(slot)[...]
+
+
+def direct_all_gather(links, ring, part, arrived=None):
+    own = part(ring.index)
+    copies = []
+    for offset in (2, 1, -1):
+        copies.append(links.send(own, own, ring.device(ring.at(offset))))
+    if arrived is not None:
+        arrived(ring.index)
+    yield
+    for copy, offset in zip(copies[1:] + copies[:1], (1, -1, 2)):
+        copy.wait_recv()
+        if arrived is not None:
+            arrived(ring.at(-offset))
 
 
 def split(value):
@@ -181,24 +232,26 @@
 
     barrier = pltpu.get_barrier_semaphore()
     friends = [twin]
-    for ring in (ring_x, ring_y, ring_z):
-        friends += [ring.device(ring.at(1)), ring.device(ring.at(-1))]
+    for ring, offsets in ((ring_x, (1, -1, 2)), (ring_y, (1, -1, 2)), (ring_z, (1, -1, 2, -2))):
+        friends += [ring.device(ring.at(offset)) for offset in offsets]
     for friend in friends:
         pl.semaphore_signal(barrier, inc=1, device_id=friend, device_id_type=MESH)
 
-    def prepare(panel, high, low, mask, first_row, first_col, pieces):
+    def prepare(panel, high, low, mask, first_row, first_col, pieces, masked=None):
         blocks, across = panel.shape[0] // BLK, panel.shape[1] // BLK
         loads[id(panel)].wait()
 
         def body(i, carry):
             rows = pl.ds(pl.multiple_of(i * BLK, BLK), BLK)
             for j in range(across):
-                kept = mask(i, j) == 1
+                kept = (mask(i, j) == 1).astype(F32)
                 if first_row is not None:
                     down, right = first_row + i, first_col + j
-                    kept = (down == right) | ((down > right) & kept)
+                    kept = jnp.where(down == right, 1.0, jnp.where(down > right, kept, 0.0))
                 columns = slice(j * BLK, (j + 1) * BLK)
-                block = panel[rows, columns] * kept.astype(F32)
+                block = panel[rows, columns] * kept
+                if masked is not None:
+                    masked[rows, columns] = block
                 top, rest = split(block)
                 high[rows, columns] = top
                 low[rows, columns] = rest
@@ -239,28 +292,53 @@
 
     middle_first = (half * n_col + col) * (p1 // 2 // n_col)
     root_first = (leaf * n_col + col) * (p2 // n_leaf // n_col)
+    rows1 = p1 // 4 // n_col
+    swap = []
+
+    def share_update():
+        here = pl.ds(pl.multiple_of(half * rows1, rows1), rows1)
+        yield from prepare(
+            ref.v_middle_update,
+            ref.h_middle_update.at[here],
+            ref.l_middle_update.at[here],
+            lambda i, j: ref.middle_updmask[0, pl.ds(i, 1), j : j + 1],
+            None,
+            None,
+            2,
+            ref.masked_update,
+        )
+        swap.append(links.send(ref.masked_update, ref.other_update, pair))
+
+    def split_other():
+        swap[0].wait_recv()
+        for start in range(0, rows1, BLK):
+            there = pl.ds(pl.multiple_of((1 - half) * rows1 + start, BLK), BLK)
+            top, rest = split(ref.other_update[start : start + BLK, :])
+            ref.h_middle_update[there, :] = top
+            ref.l_middle_update[there, :] = rest
+            yield
+
     filler = Filler()
+    filler.add(ref.masked_update, share_update())
     filler.add(ref.child_update,
-        prepare(ref.v_child_update, ref.h_child_update, ref.l_child_update, lambda i, j: ref.child_updmask[0, i, j], None, None, 1),
+        prepare(ref.v_child_update, ref.h_child_update, ref.l_child_update, lambda i, j: ref.child_updmask[0, pl.ds(i, 1), j : j + 1], None, None, 1),
     )
     filler.add(ref.hot_middle, one_hot(ref.hot_middle, child_map, middle_first, 4))
     filler.add(ref.middle_source, flip(ref.v_middle_source, ref.t_middle_source))
     filler.add(ref.middle_inverse,
         prepare(ref.v_middle_inverse, ref.h_middle_inverse, ref.l_middle_inverse,
-            lambda i, j: ref.middle_diagmask[0, i, j],
+            lambda i, j: ref.middle_diagmask[0, pl.ds(i, 1), j : j + 1],
             row * (p1 // n_row // BLK),
             lax.div(middle_first, BLK),
             4,
         ),
     )
-    filler.add(ref.middle_update,
-        prepare(ref.v_middle_update, ref.h_middle_update, ref.l_middle_update, lambda i, j: ref.middle_updmask[0, i, j], None, None, 2),
-    )
+    filler.add(ref.middle_update, split_other())
     filler.add(ref.root_source, flip(ref.v_root_source, ref.t_root_source))
     filler.add(ref.hot_root, one_hot(ref.hot_root, middle_map, root_first, 8))
     filler.add(ref.root_inverse,
         prepare(ref.v_root_inverse, ref.h_root_inverse, ref.l_root_inverse,
-            lambda i, j: ref.root_diagmask[i, j],
+            lambda i, j: ref.root_diagmask[pl.ds(i, 1), j : j + 1],
             row * (p2 // n_row // BLK),
             lax.div(root_first, BLK),
             8,
@@ -268,7 +346,7 @@
     )
 
     for _ in prepare(ref.v_child_inverse, ref.h_child_inverse, ref.l_child_inverse,
-        lambda i, j: ref.child_diagmask[0, i, j],
+        lambda i, j: ref.child_diagmask[0, pl.ds(i, 1), j : j + 1],
         row * (p0 // n_row // BLK),
         col * (p0 // n_col // BLK),
         1,
@@ -287,16 +365,12 @@
             left[width:, columns] = low
 
         def lift_reduce(lift, twin_land, land):
-            copy = links.send(lift.at[:, 1 - core], twin_land, twin)
+            copy = links.send(lift.at[:, :, 1 - core], twin_land, twin)
             yield
             copy.wait_recv()
-            lift[:, core] = lift[:, core] + twin_land[...]
-            yield from ring_reduce_scatter(
-                links,
-                ring_x,
-                longer,
-                lambda d: lift.at[d, core],
-                lambda way, step: land.at[(way + 1) // 2, step],
+            lift[:, :, core] = lift[:, :, core] + twin_land[...]
+            yield from direct_reduce_scatter(
+                links, ring_x, lambda d: lift.at[:, d, core], lambda slot: land.at[slot]
             )
 
         def row_gather(buffer):
@@ -305,9 +379,7 @@
             def arrived(d):
                 copies.append(links.send(buffer.at[d, core], buffer.at[d, core], twin))
 
-            yield from ring_all_gather(
-                links, ring_x, longer, lambda d: buffer.at[d, core], arrived
-            )
+            yield from direct_all_gather(links, ring_x, lambda d: buffer.at[d, core], arrived)
             yield
             for copy in copies:
                 copy.wait_recv()
@@ -330,17 +402,13 @@
         )
         if b == 0:
             pl.semaphore_wait(barrier, len(friends))
-        yield from ring_reduce_scatter(
-            links,
-            ring_z,
-            longer,
-            lambda d: terms.at[:, d],
-            lambda way, step: ref.child_land.at[b, (way + 1) // 2, step],
+        yield from fold_reduce_scatter(
+            links, ring_z, longer, lambda d: terms.at[:, d], lambda slot: ref.child_land.at[b, slot]
         )
         value = ref.child_value.at[b]
         value[:, col] = terms[:, col]
         ref.child_out[:, :, b] = terms[:, col].reshape(p0 // n_row // TILE, 2, mshare, TILE)
-        yield from ring_all_gather(links, ring_z, longer, lambda d: value.at[:, d])
+        yield from fold_all_gather(links, ring_z, longer, lambda d: value.at[:, d])
 
         filler.need(ref.child_update)
         for j in range(p0 // n_row // TILE):
@@ -350,14 +418,14 @@
             left,
             ref.h_child_update,
             ref.l_child_update,
-            lambda j: lift,
+            lambda j: lift.at[j],
             p0 // n_row,
             (n_x, 2, share, TILE),
         )
         yield from lift_reduce(lift, ref.child_twin.at[b], ref.child_lift_land.at[b])
 
         got = ref.child_lifts.at[b]
-        got[half, col] = lift[x, core]
+        got[half, col] = lift[0, x, core]
         copy = links.send(got.at[half, col], got.at[half, col], pair)
         filler.need(ref.hot_middle)
         total = ref.middle_total.at[b]
@@ -369,7 +437,7 @@
             for which in range(2):
                 add_block(total, got[which, d], ref.hot_middle[which * n_col + d])
 
-        yield from ring_all_gather(links, ring_z, longer, lambda d: got.at[:, d], child_arrived)
+        yield from fold_all_gather(links, ring_z, longer, lambda d: got.at[:, d], child_arrived)
         filler.need(ref.middle_source)
         rhs = ref.middle_rhs.at[b]
         source = ref.t_middle_source[pl.ds(2 * row, 2), b].reshape(share, -1)
@@ -389,60 +457,63 @@
             depth,
             (2, n_col, mshare, TILE),
         )
-        yield from ring_reduce_scatter(
-            links,
-            ring_z,
-            longer,
-            lambda d: mid.at[:, :, d],
-            lambda way, step: ref.middle_land.at[b, (way + 1) // 2, step],
+        yield from fold_reduce_scatter(
+            links, ring_z, longer, lambda d: mid.at[:, :, d], lambda slot: ref.middle_land.at[b, slot]
         )
         copy = links.send(mid.at[:, 1 - half, col], ref.middle_pair.at[b], pair)
         yield
         copy.wait_recv()
         solved = ref.middle_value.at[b]
         summed = mid[:, half, col] + ref.middle_pair[b]
-        solved[:, half, col] = summed
+        solved[:, col] = summed
         ref.middle_out[:, b] = summed
-        copy = links.send(solved.at[:, half, col], solved.at[:, half, col], pair)
-        yield
-        copy.wait_recv()
-        yield from ring_all_gather(links, ring_z, longer, lambda d: solved.at[:, :, d])
+        yield from fold_all_gather(links, ring_z, longer, lambda d: solved.at[:, d])
 
         filler.need(ref.middle_update)
+        narrow = width // 2
         for j in range(tiles):
-            fill_left(solved[j].reshape(width, TILE), slice(j * TILE, (j + 1) * TILE))
+            high, low = split(solved[j].reshape(narrow, TILE))
+            left[:narrow, j * TILE : (j + 1) * TILE] = high
+            left[narrow:width, j * TILE : (j + 1) * TILE] = low
         lift2 = ref.middle_lift.at[b]
         product(
-            left,
+            left.at[:width],
             ref.h_middle_update,
             ref.l_middle_update,
-            lambda j: lift2,
+            lambda j: lift2.at[j],
             p1 // n_row,
-            (n_x, 2, share, TILE),
+            (n_x, 2, mshare, TILE),
         )
         yield from lift_reduce(lift2, ref.middle_twin.at[b], ref.middle_lift_land.at[b])
 
         every = ref.middle_lifts.at[b]
-        every[leaf, col] = lift2[x, core]
-        yield from ring_all_gather(links, ring_y, longer, lambda d: every.at[d, col])
+        every[leaf, col] = lift2[:, x, core]
+        yield from direct_all_gather(links, ring_y, lambda d: every.at[d, col])
         filler.need(ref.hot_root)
         total2 = ref.root_total.at[b]
         total2[...] = jnp.zeros_like(total2)
 
         def middle_arrived(d):
             for which in range(n_leaf):
-                add_block(total2, every[which, d], ref.hot_root[which * n_col + d])
-
-        yield from ring_all_gather(links, ring_z, longer, lambda d: every.at[:, d], middle_arrived)
+                first, part = which // 2 * 2, which % 2
+                block = jnp.concatenate([every[first, d, part], every[first + 1, d, part]], axis=0)
+                add_block(total2, block, ref.hot_root[which * n_col + d])
+
+        yield from fold_all_gather(links, ring_z, longer, lambda d: every.at[:, d], middle_arrived)
         filler.need(ref.root_source)
         rhs2 = ref.root_rhs.at[b]
-        source2 = ref.t_root_source[pl.ds(2 * row, 2), b].reshape(share, -1)
-        rhs2[x, core] = source2 + total2[:share] + total2[share:]
+        summed2 = total2[:share] + total2[share:]
+        for part in range(2):
+            source2 = ref.t_root_source[part * n_row + row, b]
+            rhs2[x, core, part] = source2 + summed2[part * mshare : (part + 1) * mshare]
         yield from row_gather(rhs2)
 
         filler.need(ref.root_inverse)
         depth = p2 // n_leaf // n_col
-        fill_left(rhs2[...].reshape(width, depth), slice(0, depth))
+        for part in range(2):
+            high, low = split(rhs2[:, :, part].reshape(narrow, depth))
+            left[part * narrow : (part + 1) * narrow, :depth] = high
+            left[width + part * narrow : width + (part + 1) * narrow, :depth] = low
         root = ref.root_terms.at[b]
         each = p2 // n_row // TILE // n_leaf
         product(
@@ -454,19 +525,14 @@
             (n_col, cshare, TILE),
         )
         if b == 0:
-            yield from ring_reduce_scatter(
-                links,
-                ring_z,
-                longer,
-                lambda d: root.at[:, d],
-                lambda way, step: ref.root_land_az.at[(way + 1) // 2, step],
+            yield from fold_reduce_scatter(
+                links, ring_z, longer, lambda d: root.at[:, d], lambda slot: ref.root_land_az.at[slot]
             )
-            yield from ring_reduce_scatter(
+            yield from direct_reduce_scatter(
                 links,
                 ring_y,
-                longer,
                 lambda d: root.at[pl.ds(d * each, each), col],
-                lambda way, step: ref.root_land_ay.at[(way + 1) // 2, step],
+                lambda slot: ref.root_land_ay.at[slot],
             )
         else:
             yield from ring_reduce_scatter(
@@ -476,18 +542,18 @@
                 lambda d: root.at[pl.ds(d * each, each)],
                 lambda way, step: ref.root_land_by.at[b - 1, (way + 1) // 2, step],
             )
-            yield from ring_reduce_scatter(
+            yield from fold_reduce_scatter(
                 links,
                 ring_z,
                 longer,
                 lambda d: root.at[pl.ds(leaf * each, each), d],
-                lambda way, step: ref.root_land_bz.at[b - 1, (way + 1) // 2, step],
+                lambda slot: ref.root_land_bz.at[b - 1, slot],
             )
         final = ref.root_out
         mine = root[pl.ds(leaf * each, each), col]
         final[pl.ds(leaf * each, each), :, b] = mine.reshape(each, 2, mshare, TILE)
-        yield from ring_all_gather(
-            links, ring_y, longer, lambda d: final.at[pl.ds(d * each, each), :, b]
+        yield from direct_all_gather(
+            links, ring_y, lambda d: final.at[pl.ds(d * each, each), :, b]
         )
 
     run([chain(b) for b in range(BATCHES)], filler)
@@ -541,7 +607,7 @@
     width = nrhs // BATCHES
     share, cshare, mshare = width // n_row, width // n_col, width // 2 // n_col
     groups = width // mshare
-    reach_z, reach_y, reach_x = n_col // 2, n_leaf // 2, n_x // 2
+    reach_y = n_leaf // 2
     t0, t1, t2 = (p // n_row // TILE for p in (p0, p1, p2))
     scratch = dict(
         v_child_inverse=pltpu.VMEM(child_inverse.shape[-2:], F32),
@@ -554,8 +620,10 @@
         h_middle_inverse=pltpu.VMEM(middle_inverse.shape[-2:], BF16),
         l_middle_inverse=pltpu.VMEM(middle_inverse.shape[-2:], BF16),
         v_middle_update=pltpu.VMEM(middle_update.shape[-2:], F32),
-        h_middle_update=pltpu.VMEM(middle_update.shape[-2:], BF16),
-        l_middle_update=pltpu.VMEM(middle_update.shape[-2:], BF16),
+        h_middle_update=pltpu.VMEM((2 * middle_update.shape[-2], middle_update.shape[-1]), BF16),
+        l_middle_update=pltpu.VMEM((2 * middle_update.shape[-2], middle_update.shape[-1]), BF16),
+        masked_update=pltpu.VMEM(middle_update.shape[-2:], F32),
+        other_update=pltpu.VMEM(middle_update.shape[-2:], F32),
         v_root_inverse=pltpu.VMEM(root_inverse.shape[-2:], F32),
         h_root_inverse=pltpu.VMEM(root_inverse.shape[-2:], BF16),
         l_root_inverse=pltpu.VMEM(root_inverse.shape[-2:], BF16),
@@ -573,29 +641,29 @@
     scratch.update(hot_root=pltpu.VMEM((n_leaf * n_col, d2, TILE), BF16))
     shapes = dict(
         child_terms=(BATCHES, t0, n_col, cshare, TILE),
-        child_land=(BATCHES, 2, reach_z, t0, cshare, TILE),
+        child_land=(BATCHES, 7, t0, cshare, TILE),
         child_value=(BATCHES, t0, n_col, cshare, TILE),
-        child_lift=(BATCHES, n_x, 2, share, TILE),
-        child_twin=(BATCHES, n_x, share, TILE),
-        child_lift_land=(BATCHES, 2, reach_x, share, TILE),
+        child_lift=(BATCHES, 1, n_x, 2, share, TILE),
+        child_twin=(BATCHES, 1, n_x, share, TILE),
+        child_lift_land=(BATCHES, 3, 1, share, TILE),
         child_lifts=(BATCHES, 2, n_col, share, TILE),
         middle_total=(BATCHES, 2 * share, d1),
         middle_rhs=(BATCHES, n_x, 2, share, d1),
         middle_terms=(BATCHES, t1, 2, n_col, mshare, TILE),
-        middle_land=(BATCHES, 2, reach_z, t1, 2, mshare, TILE),
+        middle_land=(BATCHES, 7, t1, 2, mshare, TILE),
         middle_pair=(BATCHES, t1, mshare, TILE),
-        middle_value=(BATCHES, t1, 2, n_col, mshare, TILE),
-        middle_lift=(BATCHES, n_x, 2, share, TILE),
-        middle_twin=(BATCHES, n_x, share, TILE),
-        middle_lift_land=(BATCHES, 2, reach_x, share, TILE),
-        middle_lifts=(BATCHES, n_leaf, n_col, share, TILE),
+        middle_value=(BATCHES, t1, n_col, mshare, TILE),
+        middle_lift=(BATCHES, 2, n_x, 2, mshare, TILE),
+        middle_twin=(BATCHES, 2, n_x, mshare, TILE),
+        middle_lift_land=(BATCHES, 3, 2, mshare, TILE),
+        middle_lifts=(BATCHES, n_leaf, n_col, 2, mshare, TILE),
         root_total=(BATCHES, 2 * share, d2),
-        root_rhs=(BATCHES, n_x, 2, share, d2),
+        root_rhs=(BATCHES, n_x, 2, 2, mshare, d2),
         root_terms=(BATCHES, t2, n_col, cshare, TILE),
-        root_land_az=(2, reach_z, t2, cshare, TILE),
-        root_land_ay=(2, reach_y, t2 // n_leaf, cshare, TILE),
+        root_land_az=(7, t2, cshare, TILE),
+        root_land_ay=(3, t2 // n_leaf, cshare, TILE),
         root_land_by=(BATCHES - 1, 2, reach_y, t2 // n_leaf, n_col, cshare, TILE),
-        root_land_bz=(BATCHES - 1, 2, reach_z, t2 // n_leaf, cshare, TILE),
+        root_land_bz=(BATCHES - 1, 7, t2 // n_leaf, cshare, TILE),
     )
     for name, shape in shapes.items():
         scratch[name] = pltpu.VMEM(shape, F32)
@@ -608,12 +676,11 @@
         root_out=(t2, 2, BATCHES, mshare, TILE),
     )
     vmem = pl.BlockSpec(memory_space=pltpu.VMEM)
-    smem = pl.BlockSpec(memory_space=pltpu.SMEM)
     whole = pl.BlockSpec(memory_space=pl.ANY)
     child, middle, root = pl.pallas_call(
         functools.partial(kernel, sizes, tuple(given) + tuple(outs) + tuple(scratch)),
         out_shape=[jax.ShapeDtypeStruct(shape, F32) for shape in outs.values()],
-        in_specs=[whole] * 8 + [smem] * 5 + [vmem] * 2,
+        in_specs=[whole] * 8 + [vmem] * 7,
         out_specs=[vmem] * 3,
         scratch_shapes=list(scratch.values()),
         compiler_params=pltpu.CompilerParams(

time: 204 us -> 184 us (0.902)
  Pallas kernels: 195 us -> 176 us
    pallas_call x1, Pallas kernels: 195 us -> 176 us  [local(): pl.pallas_call(functools.partial(kernel, sizes, tuple(given) + tuple(outs...]
where the time goes in v2:
time: 184 us
  Pallas kernels  176 us (96%)
  local copies, waits for them, and re-layouts  7.56 us (4%)
    pallas_call x1, Pallas kernels, local(): pl.pallas_call(functools.partial(kernel, sizes, tuple(given) + tuple(outs...  176 us
    reshape x3, local copies, waits for them, and re-layouts, local(): blocks.reshape(*lead, blocks.shape[0], -1, TILE).swapaxes(-1, -2)  4.85 us

profile of v2, /device:TPU:2, one launch (start us, length us, event | category | flops | bytes accessed | tf_op | source)
XLA Modules:
  0.0 183.7 jit_solution(14810709872274094140)
XLA Ops:
  0.6 1.3 copy.18.refs_10_
  2.0 1.4 copy.19.refs_12_
  3.3 175.5 %shard_map.166 = (f32[2,2,3,8,256]{4,3,2,1,0:T(8,128)}, f32[4,3,8,256]{3,2,1,0:T(8,128)}, f32[8,2,3,8,256]{4,3,2,1,0:T(8,128)}) custom-call(f32[1,512,384]{2,1,0:T(8,128)} %refs_0_.1, f32[1,512,384]{2,1,0:T(8,128)} %refs_1_.1, f32[512,384]{1,0:T(8,128)} %refs_2_.1, f32[1,512,512]{2,1,0:T(8,128)} %refs_3_.1, f32[1,256,512]{2,1,0:T(8,128)} %refs_4_.1, ...), custom_call_target="tpu_custom_call" | custom-call | tf_op jit(solution)/shard_map/pallas_call | solution.py:680
  178.9 1.5 copy.23
  180.4 1.5 copy.24
  181.9 1.8 copy.25

commit v3 on v2

--- a/solution.py
+++ b/solution.py
@@ -10,7 +10,7 @@
 
 BLK = 128
 BATCHES = 3
-COPIES = 256
+COPIES = 320
 TILE = 256
 MESH = pl.DeviceIdType.MESH
 F32 = jnp.float32
@@ -26,6 +26,16 @@
                 live.remove(stream)
         if filler is not None:
             filler.step()
+
+
+def together(*streams):
+    live = list(streams)
+    while live:
+        for stream in list(live):
+            if next(stream, StopIteration) is StopIteration:
+                live.remove(stream)
+        if live:
+            yield
 
 
 class Filler:
@@ -106,6 +116,7 @@
 
 def fold_reduce_scatter(links, ring, longer, part, landing):
     before = {}
+    opposite = links.send(part(ring.at(4)), landing(6), ring.device(ring.at(2 * longer)))
     for step in range(4):
         if step > 0:
             yield
@@ -121,10 +132,6 @@
                 before[way] = links.send(
                     term, landing((way + 1) // 2 * 3 + step), ring.device(ring.at(way))
                 )
-        if step == 0:
-            opposite = links.send(
-                part(ring.at(4)), landing(6), ring.device(ring.at(2 * longer))
-            )
 
 
 def fold_all_gather(links, ring, longer, part, arrived=None):
@@ -138,11 +145,10 @@
             if step > 0:
                 before[way].wait_recv()
                 new.append(chunk)
+            if step == 2 and way == longer:
+                opposite = links.send(part(chunk), part(chunk), ring.device(ring.at(2 * way)))
             if step < 3:
                 before[way] = links.send(part(chunk), part(chunk), ring.device(ring.at(way)))
-        if step == 2:
-            chunk = ring.at(-longer * 2)
-            opposite = links.send(part(chunk), part(chunk), ring.device(ring.at(2 * longer)))
         if arrived is not None:
             for chunk in new:
                 arrived(chunk)
@@ -228,21 +234,23 @@
         )
     ):
         loads[id(landing)] = pltpu.make_async_copy(source, landing, ref.load_sems.at[index])
-        loads[id(landing)].start()
+        if index < 2:
+            loads[id(landing)].start()
 
     barrier = pltpu.get_barrier_semaphore()
     friends = [twin]
     for ring, offsets in ((ring_x, (1, -1, 2)), (ring_y, (1, -1, 2)), (ring_z, (1, -1, 2, -2))):
         friends += [ring.device(ring.at(offset)) for offset in offsets]
+    friends += [pair | ring_x.device(ring_x.at(offset)) for offset in (1, -1, 2)]
     for friend in friends:
         pl.semaphore_signal(barrier, inc=1, device_id=friend, device_id_type=MESH)
 
-    def prepare(panel, high, low, mask, first_row, first_col, pieces, masked=None):
+    def prepare(panel, high, low, mask, first_row, first_col, pieces, masked=None, unrolled=False):
         blocks, across = panel.shape[0] // BLK, panel.shape[1] // BLK
         loads[id(panel)].wait()
 
         def body(i, carry):
-            rows = pl.ds(pl.multiple_of(i * BLK, BLK), BLK)
+            rows = pl.ds(i * BLK if unrolled else pl.multiple_of(i * BLK, BLK), BLK)
             for j in range(across):
                 kept = (mask(i, j) == 1).astype(F32)
                 if first_row is not None:
@@ -258,7 +266,11 @@
             return carry
 
         for piece in range(pieces):
-            lax.fori_loop(blocks * piece // pieces, blocks * (piece + 1) // pieces, body, 0)
+            if unrolled:
+                for i in range(blocks * piece // pieces, blocks * (piece + 1) // pieces):
+                    body(i, 0)
+            else:
+                lax.fori_loop(blocks * piece // pieces, blocks * (piece + 1) // pieces, body, 0)
             yield
 
     def flip(source, flipped):
@@ -327,10 +339,11 @@
     filler.add(ref.middle_source, flip(ref.v_middle_source, ref.t_middle_source))
     filler.add(ref.middle_inverse,
         prepare(ref.v_middle_inverse, ref.h_middle_inverse, ref.l_middle_inverse,
-            lambda i, j: ref.middle_diagmask[0, pl.ds(i, 1), j : j + 1],
+            lambda i, j: ref.middle_diagmask[0, j : j + 1, i : i + 1],
             row * (p1 // n_row // BLK),
             lax.div(middle_first, BLK),
             4,
+            unrolled=True,
         ),
     )
     filler.add(ref.middle_update, split_other())
@@ -338,10 +351,11 @@
     filler.add(ref.hot_root, one_hot(ref.hot_root, middle_map, root_first, 8))
     filler.add(ref.root_inverse,
         prepare(ref.v_root_inverse, ref.h_root_inverse, ref.l_root_inverse,
-            lambda i, j: ref.root_diagmask[pl.ds(i, 1), j : j + 1],
+            lambda i, j: ref.root_diagmask[j : j + 1, i : i + 1],
             row * (p2 // n_row // BLK),
             lax.div(root_first, BLK),
             8,
+            unrolled=True,
         ),
     )
 
@@ -354,6 +368,8 @@
         pass
     for _ in flip(ref.v_child_source, ref.t_child_source):
         pass
+    for load in list(loads.values())[2:]:
+        load.start()
 
     def chain(b):
         longer = 1 if b == 1 else -1
@@ -407,7 +423,8 @@
         )
         value = ref.child_value.at[b]
         value[:, col] = terms[:, col]
-        ref.child_out[:, :, b] = terms[:, col].reshape(p0 // n_row // TILE, 2, mshare, TILE)
+        for j in range(p0 // n_row // TILE):
+            ref.child_out[:, b, :, j * TILE : (j + 1) * TILE] = terms[j, col].reshape(2, mshare, TILE)
         yield from fold_all_gather(links, ring_z, longer, lambda d: value.at[:, d])
 
         filler.need(ref.child_update)
@@ -422,16 +439,28 @@
             p0 // n_row,
             (n_x, 2, share, TILE),
         )
-        yield from lift_reduce(lift, ref.child_twin.at[b], ref.child_lift_land.at[b])
-
+        copy = links.send(lift.at[:, :, 1 - core], ref.child_twin.at[b], twin)
+        yield
+        copy.wait_recv()
+        lift[:, :, core] = lift[:, :, core] + ref.child_twin[b]
+
+        land = ref.child_lift_land.at[b]
+        copies = []
+        for slot, offset in enumerate((2, 1, -1)):
+            there = ring_x.at(offset)
+            term = lift.at[0, there, core]
+            copies.append(links.send(term, land.at[slot], ring_x.device(there)))
+            copies.append(links.send(term, land.at[slot + 3], pair | ring_x.device(there)))
+        copies.append(links.send(lift.at[0, x, core], land.at[6], pair))
         got = ref.child_lifts.at[b]
-        got[half, col] = lift[0, x, core]
-        copy = links.send(got.at[half, col], got.at[half, col], pair)
         filler.need(ref.hot_middle)
         total = ref.middle_total.at[b]
         total[...] = jnp.zeros_like(total)
         yield
-        copy.wait_recv()
+        for copy in copies:
+            copy.wait_recv()
+        got[half, col] = lift[0, x, core] + land[0] + land[1] + land[2]
+        got[1 - half, col] = land[3] + land[4] + land[5] + land[6]
 
         def child_arrived(d):
             for which in range(2):
@@ -466,7 +495,8 @@
         solved = ref.middle_value.at[b]
         summed = mid[:, half, col] + ref.middle_pair[b]
         solved[:, col] = summed
-        ref.middle_out[:, b] = summed
+        for j in range(tiles):
+            ref.middle_out[b, :, j * TILE : (j + 1) * TILE] = summed[j]
         yield from fold_all_gather(links, ring_z, longer, lambda d: solved.at[:, d])
 
         filler.need(ref.middle_update)
@@ -520,41 +550,51 @@
             left,
             ref.h_root_inverse,
             ref.l_root_inverse,
-            lambda j: root.at[j],
+            lambda j: root.at[lax.div(j, each), lax.rem(j, each)],
             depth,
             (n_col, cshare, TILE),
         )
-        if b == 0:
+        front, back = pl.ds(0, each // 2), pl.ds(each // 2, each - each // 2)
+
+        def z_first():
             yield from fold_reduce_scatter(
-                links, ring_z, longer, lambda d: root.at[:, d], lambda slot: ref.root_land_az.at[slot]
+                links,
+                ring_z,
+                longer,
+                lambda d: root.at[:, front, d],
+                lambda slot: ref.root_land_az.at[b, slot],
             )
             yield from direct_reduce_scatter(
                 links,
                 ring_y,
-                lambda d: root.at[pl.ds(d * each, each), col],
-                lambda slot: ref.root_land_ay.at[slot],
+                lambda d: root.at[d, front, col],
+                lambda slot: ref.root_land_ay.at[b, slot],
             )
-        else:
+
+        def y_first():
             yield from ring_reduce_scatter(
                 links,
                 ring_y,
                 longer,
-                lambda d: root.at[pl.ds(d * each, each)],
-                lambda way, step: ref.root_land_by.at[b - 1, (way + 1) // 2, step],
+                lambda d: root.at[d, back],
+                lambda way, step: ref.root_land_by.at[b, (way + 1) // 2, step],
             )
             yield from fold_reduce_scatter(
                 links,
                 ring_z,
-                longer,
-                lambda d: root.at[pl.ds(leaf * each, each), d],
-                lambda slot: ref.root_land_bz.at[b - 1, slot],
+                -longer,
+                lambda d: root.at[leaf, back, d],
+                lambda slot: ref.root_land_bz.at[b, slot],
             )
-        final = ref.root_out
-        mine = root[pl.ds(leaf * each, each), col]
-        final[pl.ds(leaf * each, each), :, b] = mine.reshape(each, 2, mshare, TILE)
-        yield from direct_all_gather(
-            links, ring_y, lambda d: final.at[pl.ds(d * each, each), :, b]
-        )
+
+        yield from together(y_first(), z_first())
+        final = ref.root_final.at[b]
+        final[leaf] = root[leaf, :, col]
+        yield from direct_all_gather(links, ring_y, lambda d: final.at[d])
+        for d in range(n_leaf):
+            for j in range(each):
+                columns = slice((d * each + j) * TILE, (d * each + j + 1) * TILE)
+                ref.root_out[:, b, :, columns] = final[d, j].reshape(2, mshare, TILE)
 
     run([chain(b) for b in range(BATCHES)], filler)
     assert links.count <= COPIES
@@ -581,6 +621,8 @@
     child_rowmap,
     middle_rowmap,
 ):
+    middle_diagmask = middle_diagmask.swapaxes(1, 2)
+    root_diagmask = root_diagmask.T
     given = dict(
         child_source=child_source,
         middle_source=middle_source,
@@ -645,7 +687,7 @@
         child_value=(BATCHES, t0, n_col, cshare, TILE),
         child_lift=(BATCHES, 1, n_x, 2, share, TILE),
         child_twin=(BATCHES, 1, n_x, share, TILE),
-        child_lift_land=(BATCHES, 3, 1, share, TILE),
+        child_lift_land=(BATCHES, 7, share, TILE),
         child_lifts=(BATCHES, 2, n_col, share, TILE),
         middle_total=(BATCHES, 2 * share, d1),
         middle_rhs=(BATCHES, n_x, 2, share, d1),
@@ -659,11 +701,12 @@
         middle_lifts=(BATCHES, n_leaf, n_col, 2, mshare, TILE),
         root_total=(BATCHES, 2 * share, d2),
         root_rhs=(BATCHES, n_x, 2, 2, mshare, d2),
-        root_terms=(BATCHES, t2, n_col, cshare, TILE),
-        root_land_az=(7, t2, cshare, TILE),
-        root_land_ay=(3, t2 // n_leaf, cshare, TILE),
-        root_land_by=(BATCHES - 1, 2, reach_y, t2 // n_leaf, n_col, cshare, TILE),
-        root_land_bz=(BATCHES - 1, 7, t2 // n_leaf, cshare, TILE),
+        root_terms=(BATCHES, n_leaf, t2 // n_leaf, n_col, cshare, TILE),
+        root_final=(BATCHES, n_leaf, t2 // n_leaf, cshare, TILE),
+        root_land_az=(BATCHES, 7, n_leaf, t2 // n_leaf // 2, cshare, TILE),
+        root_land_ay=(BATCHES, 3, t2 // n_leaf // 2, cshare, TILE),
+        root_land_by=(BATCHES, 2, reach_y, t2 // n_leaf // 2, n_col, cshare, TILE),
+        root_land_bz=(BATCHES, 7, t2 // n_leaf // 2, cshare, TILE),
     )
     for name, shape in shapes.items():
         scratch[name] = pltpu.VMEM(shape, F32)
@@ -671,9 +714,9 @@
     scratch.update(recv_sems=pltpu.SemaphoreType.DMA((COPIES,)))
     scratch.update(load_sems=pltpu.SemaphoreType.DMA((8,)))
     outs = dict(
-        child_out=(t0, 2, BATCHES, mshare, TILE),
-        middle_out=(t1, BATCHES, mshare, TILE),
-        root_out=(t2, 2, BATCHES, mshare, TILE),
+        child_out=(2, BATCHES, mshare, t0 * TILE),
+        middle_out=(BATCHES, mshare, t1 * TILE),
+        root_out=(2, BATCHES, mshare, t2 * TILE),
     )
     vmem = pl.BlockSpec(memory_space=pltpu.VMEM)
     whole = pl.BlockSpec(memory_space=pl.ANY)
@@ -687,11 +730,10 @@
             collective_id=0, has_side_effects=True, vmem_limit_bytes=60 * 2**20
         ),
     )(*given.values())
-    return tuple(
-        blocks.reshape(*lead, blocks.shape[0], -1, TILE)
-        .swapaxes(-1, -2)
-        .reshape(*lead, blocks.shape[0] * TILE, -1)
-        for blocks, lead in ((child, (1,)), (middle, (1,)), (root, ()))
+    return (
+        child.reshape(1, nrhs // n_col, -1).swapaxes(1, 2),
+        middle.reshape(1, nrhs // 2 // n_col, -1).swapaxes(1, 2),
+        root.reshape(nrhs // n_col, -1).T,
     )
 
 

time: 184 us -> 179 us (0.973)
  Pallas kernels: 176 us -> 173 us
  local copies, waits for them, and re-layouts: 7.56 us -> 4.84 us
    reshape x3 -> x0, local copies, waits for them, and re-layouts: 4.85 us -> none  [local(): blocks.reshape(*lead, blocks.shape[0], -1, TILE).swapaxes(-1, -2)]
    pallas_call x1, Pallas kernels: 176 us -> 173 us  [local(): pl.pallas_call(functools.partial(kernel, sizes, tuple(given) + tuple(outs...]
    unnamed x2 -> x3, local copies, waits for them, and re-layouts: 2.7 us -> 4.84 us
where the time goes in v3:
time: 179 us
  Pallas kernels  173 us (97%)
  local copies, waits for them, and re-layouts  4.84 us (3%)
    pallas_call x1, Pallas kernels, local(): pl.pallas_call(functools.partial(kernel, sizes, tuple(given) + tuple(outs...  173 us
    unnamed x3, local copies, waits for them, and re-layouts  4.84 us

profile of v3, /device:TPU:2, one launch (start us, length us, event | category | flops | bytes accessed | tf_op | source)
XLA Modules:
  0.0 178.7 jit_solution(17486353256395880527)
XLA Ops:
  0.6 173.3 %shard_map.166 = (f32[2,3,8,512]{3,2,1,0:T(8,128)}, f32[3,8,1024]{2,1,0:T(8,128)}, f32[2,3,8,2048]{3,2,1,0:T(8,128)}) custom-call(f32[1,512,384]{2,1,0:T(8,128)} %refs_0_.1, f32[1,512,384]{2,1,0:T(8,128)} %refs_1_.1, f32[512,384]{1,0:T(8,128)} %refs_2_.1, f32[1,512,512]{2,1,0:T(8,128)} %refs_3_.1, f32[1,256,512]{2,1,0:T(8,128)} %refs_4_.1, ...), custom_call_target="tpu_custom_call" | custom-call | tf_op jit(solution)/shard_map/pallas_call | solution.py:723
  173.9 1.5 copy.21
  175.4 1.5 copy.22
  177.0 1.8 copy.23

commit v4 on v3

--- a/solution.py
+++ b/solution.py
@@ -86,13 +86,14 @@
 
 
 class Ring:
-    def __init__(self, index, length, device):
+    def __init__(self, index, length, device, sense=1):
         self.index = index
         self.length = length
         self.device = device
+        self.sense = sense
 
     def at(self, offset):
-        return lax.rem(self.index + offset + 2 * self.length, self.length)
+        return lax.rem(self.index + self.sense * offset + 2 * self.length, self.length)
 
 
 def ring_reduce_scatter(links, ring, longer, part, landing):
@@ -210,8 +211,8 @@
     leaf, row, col = lax.axis_index("leaf"), lax.axis_index("row"), lax.axis_index("col")
     half, couple = lax.rem(leaf, 2), lax.div(leaf, 2)
     x, core = lax.div(row, 2), lax.rem(row, 2)
-    ring_y = Ring(leaf, n_leaf, lambda i: {"leaf": i})
-    ring_z = Ring(col, n_col, lambda i: {"col": i})
+    ring_y = Ring(leaf, n_leaf, lambda i: {"leaf": i}, 1 - 2 * core)
+    ring_z = Ring(col, n_col, lambda i: {"col": i}, 1 - 2 * core)
     ring_x = Ring(x, n_x, lambda i: {"row": i * 2 + core})
     pair = {"leaf": couple * 2 + 1 - half}
     twin = {"row": x * 2 + 1 - core}

time: 179 us -> 177 us (0.989)
  no operation moved by 1% of the time
where the time goes in v4:
time: 177 us
  Pallas kernels  172 us (97%)
  local copies, waits for them, and re-layouts  4.84 us (3%)
    pallas_call x1, Pallas kernels, local(): pl.pallas_call(functools.partial(kernel, sizes, tuple(given) + tuple(outs...  172 us
    unnamed x3, local copies, waits for them, and re-layouts  4.84 us

profile of v4, /device:TPU:2, one launch (start us, length us, event | category | flops | bytes accessed | tf_op | source)
XLA Modules:
  0.0 177.2 jit_solution(8710376916101148639)
XLA Ops:
  0.6 171.7 %shard_map.166 = (f32[2,3,8,512]{3,2,1,0:T(8,128)}, f32[3,8,1024]{2,1,0:T(8,128)}, f32[2,3,8,2048]{3,2,1,0:T(8,128)}) custom-call(f32[1,512,384]{2,1,0:T(8,128)} %refs_0_.1, f32[1,512,384]{2,1,0:T(8,128)} %refs_1_.1, f32[512,384]{1,0:T(8,128)} %refs_2_.1, f32[1,512,512]{2,1,0:T(8,128)} %refs_3_.1, f32[1,256,512]{2,1,0:T(8,128)} %refs_4_.1, ...), custom_call_target="tpu_custom_call" | custom-call | tf_op jit(solution)/shard_map/pallas_call | solution.py:724
  172.4 1.5 copy.21
  173.9 1.5 copy.22
  175.4 1.8 copy.23
